TPU v7x, 512 devices: a whole 4x4x16 slice. The times are simulated.
512 devices in a mesh: ctx: 64 (over y, z), head: 8 (over x, core).
Axes of the slice: x: 4, y: 4, z: 16, core: 2. Of those that a mesh axis runs over, the one named last changes fastest.
Arguments:
- query_rows: bfloat16 [8, 65536, 8, 128], P('head', 'ctx'), may hold values from -64 to 64
- key_rows: bfloat16 [8, 262144, 128], P('head', 'ctx'), may hold values from -80 to 80
- value_rows: bfloat16 [8, 262144, 128], P('head', 'ctx'), may hold values from -20 to 20
Outputs:
- key_scores: float32 [8, 262144], P('head', 'ctx')
All inputs are finite; a program needn't handle non-finite values.
Results may differ from a plain program's by a relative error of at most 0.0003.
Values may be sent and summed in bfloat16 or wider, within the bound.
A program may use at most 128 MiB of HBM per device.

v0:
```python
import math

import jax
import jax.numpy as jnp
from jax import lax
from jax.sharding import PartitionSpec as P


def score_keys(scoring_keys, covariance, center):
    feature = scoring_keys.shape[-1]
    key_float = scoring_keys.astype(jnp.float32)
    results = []
    for member in range(covariance.shape[0]):
        projected = jnp.einsum(
            "gtd,gde->gte", key_float, covariance[member], precision=lax.Precision.HIGHEST
        )
        quadratic = jnp.sum(projected * key_float, axis=-1)
        linear = jnp.einsum(
            "gtd,gd->gt", key_float, center[member], precision=lax.Precision.HIGHEST
        )
        results.append(linear / math.sqrt(feature) + quadratic / (2.0 * feature))
    return jnp.stack(results)


def local(query_rows, key_rows, value_rows):
    rep_local, query_count, groups, feature = query_rows.shape
    ones_column = jnp.ones((query_count,), jnp.bfloat16)
    moment_two = jnp.einsum(
        "rtgd,rtge->rgde", query_rows, query_rows, preferred_element_type=jnp.float32
    )
    moment_one = jnp.einsum(
        "rtgd,t->rgd", query_rows, ones_column, preferred_element_type=jnp.float32
    )
    moment_two, moment_one = lax.psum((moment_two, moment_one), "ctx")
    moment_two, moment_one = (
        lax.all_to_all(moment_two, "head", split_axis=1, concat_axis=0, tiled=True),
        lax.all_to_all(moment_one, "head", split_axis=1, concat_axis=0, tiled=True),
    )
    count_total = query_count * lax.axis_size("ctx")
    center = moment_one / count_total
    covariance = moment_two / count_total - center[..., :, None] * center[..., None, :]
    exponent = score_keys(key_rows, covariance, center)
    local_peak = jnp.max(exponent, axis=-1)
    highest = lax.pmax(local_peak, "ctx")
    mass = lax.psum(jnp.sum(jnp.exp(exponent - highest[..., None]), axis=-1), "ctx")
    weights = jnp.exp(exponent - highest[..., None]) / mass[..., None]
    share = jnp.sum(weights, axis=0)
    square_sum = jnp.einsum(
        "gtd,gtd->gt", value_rows, value_rows, preferred_element_type=jnp.float32
    )
    value_scale = jnp.sqrt(square_sum / feature + 1e-06)
    key_total = key_rows.shape[1] * lax.axis_size("ctx")
    rep_total = query_rows.shape[0] * lax.axis_size("head")
    return key_total / rep_total * share * value_scale


def solution(mesh):
    in_specs = (P("head", "ctx", None, None), P("head", "ctx", None), P("head", "ctx", None))
    out_specs = P("head", "ctx")
    return jax.shard_map(local, mesh=mesh, in_specs=in_specs, out_specs=out_specs, check_vma=False)
```

profile of v0, /device:TPU:32, one launch (start us, length us, event | category | flops | bytes accessed | tf_op | source)
XLA Modules:
  0.0 733.2 jit_solution(2185675900662063278)
XLA Ops:
  6.5 2.1 fusion.1
  8.7 146.2 %psum.23 = f32[1,8,128]{2,0,1:T(1,128)} all-reduce(f32[1,8,128]{2,0,1:T(1,128)S(1)} %fusion.1), channel_id=1, replica_groups=mesh['ctx'=64,'head'=8] {'ctx'}, use_global_device_ids=true, to_apply=%region_0.0 | all-reduce | flops 1024 | bytes 8192 | tf_op jit(solution)/shard_map/psum | solution.py:34
  154.9 4.3 all-to-all-start
  159.3 2.1 fusion.13
  161.9 2.5 all-to-all-done
  165.3 0.9 fusion.32
  166.2 0.9 fusion.29
  167.2 0.9 fusion.26
  168.1 0.9 fusion.23
  169.0 0.9 fusion.20
  169.9 251.5 %all-reduce.2.cloned.1.call-done = f32[1,8,128,128]{3,2,1,0:T(8,128)} async-done(((f32[1,8,128,128]{3,2,1,0:T(8,128)}), f32[1,8,128,128]{3,2,1,0:T(8,128)}) %all-reduce.2.cloned.1.call-update) | async-done | bytes 524304 | tf_op jit(solution)/shard_map/psum | solution.py:34
  421.5 4.3 all-to-all-start.1
  426.6 0.9 fusion.38
  427.5 8.5 %all-to-all-done.1 = f32[1,8,128,128]{3,2,0,1:T(8,128)S(1)} async-done(((f32[1,8,128,128]{3,2,0,1:T(8,128)}), f32[1,8,128,128]{3,2,0,1:T(8,128)S(1)}, u32[]{:S(2)}, u32[]{:S(2)}) %all-to-all-start.1) | async-done | bytes 524320 | tf_op jit(solution)/shard_map/all_to_all | solution.py:36
  436.3 1.1 fusion.6
  437.4 1.1 fusion.7
  438.5 1.1 fusion.8
  439.7 1.1 fusion.9
  440.8 1.1 fusion.10
  441.9 1.1 fusion.11
  443.1 1.1 fusion.12
  444.2 1.1 fusion.5
  445.8 139.3 %pmax.10 = f32[8]{0:T(128)S(1)} all-reduce(f32[8]{0:T(128)S(1)} %reduce_max.11), channel_id=1, replica_groups=mesh['ctx'=64,'head'=8] {'ctx'}, use_global_device_ids=true, to_apply=%region_11.0 | all-reduce | flops 8 | bytes 64 | tf_op jit(solution)/shard_map/pmax | solution.py:44
  586.0 139.6 %psum.26 = f32[8]{0:T(128)S(1)} all-reduce(f32[8]{0:T(128)S(1)} %fusion.40), channel_id=1, replica_groups=mesh['ctx'=64,'head'=8] {'ctx'}, use_global_device_ids=true, to_apply=%region_13.0 | all-reduce | flops 8 | bytes 64 | tf_op jit(solution)/shard_map/psum | solution.py:45
  (27 shorter events, 4.6 us)
Async XLA Ops:
  6.5 152.7 %copy-start.1 = (bf16[1,1024,8,128]{3,2,1,0:T(8,128)(2,1)S(1)}, bf16[1,1024,8,128]{3,2,1,0:T(8,128)(2,1)}, u32[]{:S(2)}) copy-start(bf16[1,1024,8,128]{3,2,1,0:T(8,128)(2,1)} %param.3) | copy-start | bytes 6291460
  154.9 9.5 %all-to-all-start = ((f32[1,8,128]{2,0,1:T(1,128)}), f32[1,8,128]{2,0,1:T(1,128)S(1)}, u32[]{:S(2)}, u32[]{:S(2)}) async-start(f32[1,8,128]{2,0,1:T(1,128)} %psum.23), calls=%async_computation | async-start | bytes 8192 | tf_op jit(solution)/shard_map/all_to_all | solution.py:37
  159.2 2.2 copy-start
  159.2 262.2 %all-reduce.2.cloned.1.call-start = ((), (), s32[]{:S(2)}) async-start(), calls=%async_computation.2 | async-start | bytes 1048576 | tf_op jit(solution)/shard_map/psum | solution.py:34
  421.5 14.6 %all-to-all-start.1 = ((f32[1,8,128,128]{3,2,0,1:T(8,128)}), f32[1,8,128,128]{3,2,0,1:T(8,128)S(1)}, u32[]{:S(2)}, u32[]{:S(2)}) async-start(f32[1,8,128,128]{3,2,0,1:T(8,128)} %bitcast.191), calls=%async_computation.1 | async-start | bytes 1048576 | tf_op jit(solution)/shard_map/all_to_all | solution.py:36
  444.2 141.2 %copy-start.2 = (bf16[1,4096,128]{2,1,0:T(8,128)(2,1)S(1)}, bf16[1,4096,128]{2,1,0:T(8,128)(2,1)}, u32[]{:S(2)}) copy-start(bf16[1,4096,128]{2,1,0:T(8,128)(2,1)} %param.5) | copy-start | bytes 3145732
Sparse Core Ops, SparseCore 0:
  163.5 257.9 all-reduce.1
where the time goes:
time: 733 us
  blocking collectives  425 us (58%)
  waiting for transfers between devices  263 us (36%)
  matrix products  20.6 us (3%)
  between operations  13.6 us (2%)
  starting transfers between devices  8.6 us (1%)
    psum x1, waiting for transfers between devices, local(): moment_two, moment_one = lax.psum((moment_two, moment_one), 'ctx')  252 us
    psum x1, blocking collectives, local(): moment_two, moment_one = lax.psum((moment_two, moment_one), 'ctx')  146 us
    psum x1, blocking collectives, local(): lax.psum(jnp.sum(jnp.exp(exponent - highest[..., None]), axis=-1), 'ctx')  140 us
    pmax x1, blocking collectives, local(): highest = lax.pmax(local_peak, 'ctx')  139 us
  transfers between devices with their start and end apart: 3, of which 3 were waited for; matrix products, arithmetic and copies ran while one was open for 1% of the time, Pallas kernels for 0%

commit v1 on v0

v1 whole, which is shorter than its diff:
```python
import functools
import math

import jax
import jax.numpy as jnp
from jax import lax
from jax.experimental import pallas as pl
from jax.experimental.pallas import tpu as pltpu
from jax.sharding import PartitionSpec as P

MESH = pl.DeviceIdType.MESH
F32 = jnp.float32
BF16 = jnp.bfloat16

NY, NZ, NH = 4, 16, 8
DH = 128
HALF = DH // 2
REP = 8
ROWS = 9
FAR_FIRST = (8, 7, 9, 6, 10, 5, 11, 4, 12, 3, 13, 2, 14, 1, 15)


def split_two(value):
    high = value.astype(BF16)
    low = (value - high.astype(F32)).astype(BF16)
    return high, low


def kernel(
    query_count, key_count,
    q_hbm, k_hbm, v_hbm, out_ref,
    q_in, k_in, v_in, q_f32, packed, plane, line, part, full, weights, keys_t, scale,
    expo, mass, in_sem, send_sem, recv_sem,
):
    ctx = lax.axis_index("ctx")
    head = lax.axis_index("head")
    y = lax.div(ctx, NZ)
    z = lax.rem(ctx, NZ)

    load_q = pltpu.make_async_copy(q_hbm, q_in, in_sem.at[0])
    load_k = pltpu.make_async_copy(k_hbm, k_in, in_sem.at[1])
    load_v = pltpu.make_async_copy(v_hbm, v_in, in_sem.at[2])
    load_q.start()
    load_k.start()
    load_v.start()

    plane_peers = [
        (lax.rem(y + dy, NY), lax.rem(head + dh, NH))
        for dy in range(NY)
        for dh in range(NH)
        if (dy, dh) != (0, 0)
    ]
    line_peers = [lax.rem(z + dz, NZ) for dz in FAR_FIRST]

    barrier = pltpu.get_barrier_semaphore()
    for zz in line_peers:
        pl.semaphore_signal(barrier, inc=1, device_id=(y * NZ + zz, head), device_id_type=MESH)
    for yy, hh in plane_peers:
        pl.semaphore_signal(barrier, inc=1, device_id=(yy * NZ + z, hh), device_id_type=MESH)

    load_q.wait()
    step = 64

    def widen(t, _):
        rows = q_in[0, pl.ds(t * step, step)].astype(F32)
        q_f32[pl.ds(t * step * NH, step * NH), :] = rows.reshape(step * NH, DH)
        return 0

    lax.fori_loop(0, query_count // step, widen, 0)
    row = lax.broadcasted_iota(jnp.int32, (HALF, DH), 0)
    lane = lax.broadcasted_iota(jnp.int32, (HALF, DH), 1)
    for g in range(NH):
        rows = q_f32[pl.ds(g, query_count, stride=NH), :]
        first = jnp.sum(rows, axis=0, keepdims=True)
        narrow = rows.astype(BF16)
        second = lax.dot_general(
            narrow, narrow, (((0,), (0,)), ((), ())), preferred_element_type=F32
        )
        top = second[:HALF]
        bottom = pltpu.roll(second[HALF:], HALF, 1)
        both = jnp.where(lane < row, bottom, top)
        diagonal = jnp.sum(jnp.where(lane == row, bottom, 0.0), axis=0, keepdims=True)
        for q in range(NY):
            for h in range(2):
                at = q * 16 + h * 8
                packed[g, q, h, 0:8, :] = both[at : at + 8]
            packed[g, q, 0, 8:9, :] = first
            packed[g, q, 1, 8:9, :] = diagonal

    pl.semaphore_wait(barrier, len(plane_peers) + len(line_peers))

    def copy(src, dst, phase, device):
        return pltpu.make_async_remote_copy(
            src_ref=src, dst_ref=dst, send_sem=send_sem.at[phase], recv_sem=recv_sem.at[phase],
            device_id=device, device_id_type=MESH,
        )

    def wait(ref, sem):
        pltpu.make_async_copy(ref, ref, sem).wait()

    for yy, hh in plane_peers:
        copy(
            packed.at[hh, yy, :, pl.ds(0, ROWS)],
            plane.at[pl.ds(y * 16 + 2 * head, 2), pl.ds(0, ROWS)],
            0, (yy * NZ + z, hh),
        ).start()
    plane[pl.ds(y * 16 + 2 * head, 2), 0:ROWS, :] = packed[head, y, :, 0:ROWS, :]

    load_k.wait()
    wide = 512

    def turn_keys(t, _):
        turned = k_in[0, pl.ds(t * wide, wide), :].astype(F32).T.astype(BF16)
        keys_t[0:DH, pl.ds(t * wide, wide)] = turned
        keys_t[DH : 2 * DH, pl.ds(t * wide, wide)] = turned
        return 0

    lax.fori_loop(0, key_count // wide, turn_keys, 0)

    wait(plane.at[pl.ds(0, 62), pl.ds(0, ROWS)], recv_sem.at[0])
    total = plane[0:16, 0:ROWS, :]
    for yy in range(1, NY):
        total = total + plane[yy * 16 : yy * 16 + 16, 0:ROWS, :]
    line[:, 0:ROWS, :] = total

    for zz in line_peers:
        copy(line.at[zz, pl.ds(0, ROWS)], part.at[z, pl.ds(0, ROWS)], 1, (y * NZ + zz, head)).start()
    part[z, 0:ROWS, :] = line[z, 0:ROWS, :]

    load_v.wait()

    def scale_values(t, _):
        turned = v_in[0, pl.ds(t * wide, wide), :].astype(F32).T
        squares = jnp.sum(turned * turned, axis=0, keepdims=True)
        scale[:, pl.ds(t * wide, wide)] = jnp.sqrt(squares / DH + 1e-06)
        return 0

    lax.fori_loop(0, key_count // wide, scale_values, 0)

    wait(part.at[pl.ds(0, 15), pl.ds(0, ROWS)], recv_sem.at[1])
    total = part[0, 0:ROWS, :]
    for zz in range(1, NZ):
        total = total + part[zz, 0:ROWS, :]
    mine = y * 16 + z
    full[mine, 0:ROWS, :] = total

    for zz in line_peers:
        here = full.at[mine, pl.ds(0, ROWS)]
        copy(here, here, 2, (y * NZ + zz, head)).start()
    wait(full.at[pl.ds(0, 15), pl.ds(0, ROWS)], recv_sem.at[2])

    for dy in range(1, NY):
        here = full.at[pl.ds(y * 16, 16), pl.ds(0, 8)]
        copy(here, here, 3, (lax.rem(y + dy, NY) * NZ + z, head)).start()
    extra = full[pl.ds(y * 16, 16), 8, :] * (1.0 / (query_count * NY * NZ))
    columns = extra.T
    wait(full.at[pl.ds(0, 48), pl.ds(0, 8)], recv_sem.at[3])

    for r in range(REP):
        quarters = [full[q * 16 + 2 * r + h, 0:8, :] for q in range(NY) for h in range(2)]
        moments = jnp.concatenate(quarters, axis=0) * (1.0 / (query_count * NY * NZ))
        center = extra[2 * r : 2 * r + 1, :]
        up = columns[0:HALF, 2 * r : 2 * r + 1]
        down = columns[HALF:DH, 2 * r : 2 * r + 1]
        diagonal = columns[0:HALF, 2 * r + 1 : 2 * r + 2]
        below = lane < row
        value = moments - jnp.where(below, down * pltpu.roll(center, HALF, 1), up * center)
        value = value * (1.0 / (2.0 * DH))
        corner = (diagonal - down * down) * (1.0 / (2.0 * DH))
        on = lane == row
        upper = jnp.where(below, 0.0, jnp.where(on, value, 2.0 * value))
        lower = jnp.where(below, 2.0 * value, jnp.where(on, corner, 0.0))
        for at, block in ((0, upper), (HALF, pltpu.roll(lower, HALF, 1))):
            high, low = split_two(block)
            weights[r * DH + at : r * DH + at + HALF, 0:DH] = high
            weights[r * DH + at : r * DH + at + HALF, DH : 2 * DH] = low
    high, low = split_two(extra * (1.0 / math.sqrt(DH)))
    weights[REP * DH : REP * DH + 16, 0:DH] = high
    weights[REP * DH : REP * DH + 16, DH : 2 * DH] = low

    tile = 256

    def score(t, _):
        keys = keys_t[:, pl.ds(t * tile, tile)]
        keys_f32 = keys[0:DH].astype(F32)
        projected = jnp.dot(weights[...], keys, preferred_element_type=F32)
        for r in range(REP):
            quadratic = jnp.sum(projected[r * DH : (r + 1) * DH] * keys_f32, axis=0, keepdims=True)
            linear = projected[REP * DH + 2 * r : REP * DH + 2 * r + 1]
            expo[r : r + 1, pl.ds(t * tile, tile)] = quadratic + linear
        return 0

    lax.fori_loop(0, key_count // tile, score, 0)

    exponent = expo[...]
    peak = jnp.max(exponent, axis=1, keepdims=True)
    grown = jnp.exp(exponent - peak)
    expo[...] = grown
    local = jnp.sum(grown, axis=1, keepdims=True)
    row8 = lax.broadcasted_iota(jnp.int32, (REP, DH), 0)
    lane8 = lax.broadcasted_iota(jnp.int32, (REP, DH), 1)
    note = jnp.where(lane8 == row8, peak, jnp.where(lane8 == row8 + REP, local, 0.0))
    mass[pl.ds(ctx, 1), :] = jnp.sum(note, axis=0, keepdims=True)
    for dz in FAR_FIRST + (0,):
        for dy in (2, 1, 3, 0):
            if (dy, dz) != (0, 0):
                here = mass.at[pl.ds(ctx, 1)]
                copy(here, here, 4, (lax.rem(y + dy, NY) * NZ + lax.rem(z + dz, NZ), head)).start()
    wait(mass.at[pl.ds(0, 63)], recv_sem.at[4])
    notes = mass[...]
    highest = jnp.max(notes, axis=0, keepdims=True)
    sums = pltpu.roll(notes, DH - REP, 1)
    inside = lax.broadcasted_iota(jnp.int32, notes.shape, 1) < REP
    terms = jnp.where(inside, sums * jnp.exp(jnp.where(inside, notes - highest, 0.0)), 0.0)
    denominator = jnp.sum(terms, axis=0, keepdims=True)
    pick = lane8 == row8
    highest_col = jnp.sum(jnp.where(pick, highest, 0.0), axis=1, keepdims=True)
    denominator_col = jnp.sum(jnp.where(pick, denominator, 0.0), axis=1, keepdims=True)
    factor = jnp.exp(peak - highest_col) / denominator_col
    share = jnp.sum(expo[...] * factor, axis=0, keepdims=True)
    out_ref[...] = share * scale[...] * (key_count * NY * NZ / REP)

    wait(plane.at[pl.ds(0, 62), pl.ds(0, ROWS)], send_sem.at[0])
    wait(part.at[pl.ds(0, 15), pl.ds(0, ROWS)], send_sem.at[1])
    wait(full.at[pl.ds(0, 15), pl.ds(0, ROWS)], send_sem.at[2])
    wait(full.at[pl.ds(0, 48), pl.ds(0, 8)], send_sem.at[3])
    wait(mass.at[pl.ds(0, 63)], send_sem.at[4])


def local(query_rows, key_rows, value_rows):
    query_count = query_rows.shape[1]
    key_count = key_rows.shape[1]
    any_space = pl.BlockSpec(memory_space=pl.ANY)
    return pl.pallas_call(
        functools.partial(kernel, query_count, key_count),
        out_shape=jax.ShapeDtypeStruct((1, key_count), F32),
        in_specs=[any_space] * 3,
        out_specs=pl.BlockSpec(memory_space=pltpu.VMEM),
        scratch_shapes=[
            pltpu.VMEM(query_rows.shape, BF16),
            pltpu.VMEM(key_rows.shape, BF16),
            pltpu.VMEM(value_rows.shape, BF16),
            pltpu.VMEM((query_count * NH, DH), F32),
            pltpu.VMEM((NH, NY, 2, 16, DH), F32),
            pltpu.VMEM((NY * 16, 16, DH), F32),
            pltpu.VMEM((NZ, 16, DH), F32),
            pltpu.VMEM((NZ, 16, DH), F32),
            pltpu.VMEM((NY * 16, 16, DH), F32),
            pltpu.VMEM((REP * DH + 16, 2 * DH), BF16),
            pltpu.VMEM((2 * DH, key_count), BF16),
            pltpu.VMEM((1, key_count), F32),
            pltpu.VMEM((REP, key_count), F32),
            pltpu.VMEM((NY * NZ, DH), F32),
            pltpu.SemaphoreType.DMA((3,)),
            pltpu.SemaphoreType.DMA((5,)),
            pltpu.SemaphoreType.DMA((5,)),
        ],
        compiler_params=pltpu.CompilerParams(
            collective_id=0, has_side_effects=True, vmem_limit_bytes=48 << 20
        ),
    )(query_rows, key_rows, value_rows)


def solution(mesh):
    in_specs = (P("head", "ctx", None, None), P("head", "ctx", None), P("head", "ctx", None))
    return jax.shard_map(
        local, mesh=mesh, in_specs=in_specs, out_specs=P("head", "ctx"), check_vma=False
    )
```

time: 733 us -> 60.6 us (0.08)
  the two profiles are of different devices: /device:TPU:32 before, /device:TPU:2 now
where the time goes in v1:
time: 60.6 us; the launch traced here: 60.2 us
  Pallas kernels  55.6 us (92%)
  local copies, waits for them, and re-layouts  4.65 us (8%)
    pallas_call x1, Pallas kernels, local(): pl.pallas_call(functools.partial(kernel, query_count, key_count), out_sha...  55.6 us
    unnamed x7, local copies, waits for them, and re-layouts  4.65 us

profile of v1, /device:TPU:2, one launch (start us, length us, event | category | flops | bytes accessed | tf_op | source)
XLA Modules:
  0.0 60.2 jit_solution(4187067874215299932)
XLA Ops:
  0.0 0.0 copy-start
  0.0 1.6 %copy-done = bf16[1,1024,8,128]{3,2,1,0:T(8,128)(2,1)S(1)} copy-done((bf16[1,1024,8,128]{3,2,1,0:T(8,128)(2,1)S(1)}, bf16[1,1024,8,128]{3,2,1,0:T(8,128)(2,1)}, u32[]{:S(2)}) %copy-start) | copy-done | bytes 2097176
  1.6 0.0 copy-start.1
  1.6 1.2 %copy-done.1 = bf16[1,4096,128]{2,1,0:T(8,128)(2,1)S(1)} copy-done((bf16[1,4096,128]{2,1,0:T(8,128)(2,1)S(1)}, bf16[1,4096,128]{2,1,0:T(8,128)(2,1)}, u32[]{:S(2)}) %copy-start.1) | copy-done | bytes 1048600
  2.8 0.0 copy-start.2
  2.8 1.2 %copy-done.2 = bf16[1,4096,128]{2,1,0:T(8,128)(2,1)S(1)} copy-done((bf16[1,4096,128]{2,1,0:T(8,128)(2,1)S(1)}, bf16[1,4096,128]{2,1,0:T(8,128)(2,1)}, u32[]{:S(2)}) %copy-start.2) | copy-done | bytes 1048600
  4.0 55.6 %shard_map.37 = f32[1,4096]{1,0:T(1,128)S(1)} custom-call(bf16[1,1024,8,128]{3,2,1,0:T(8,128)(2,1)S(1)} %copy-done, bf16[1,4096,128]{2,1,0:T(8,128)(2,1)S(1)} %copy-done.1, bf16[1,4096,128]{2,1,0:T(8,128)(2,1)S(1)} %copy-done.2), custom_call_target="tpu_custom_call" | custom-call | tf_op jit(solution)/shard_map/pallas_call | solution.py:234
  59.6 0.6 %copy.5 = f32[1,4096]{1,0:T(1,128)} copy(f32[1,4096]{1,0:T(1,128)S(1)} %shard_map.37) | data formatting | bytes 32768
Async XLA Ops:
  0.0 1.6 %copy-start = (bf16[1,1024,8,128]{3,2,1,0:T(8,128)(2,1)S(1)}, bf16[1,1024,8,128]{3,2,1,0:T(8,128)(2,1)}, u32[]{:S(2)}) copy-start(bf16[1,1024,8,128]{3,2,1,0:T(8,128)(2,1)} %q_hbm.1) | copy-start | bytes 6291460
  1.6 1.2 %copy-start.1 = (bf16[1,4096,128]{2,1,0:T(8,128)(2,1)S(1)}, bf16[1,4096,128]{2,1,0:T(8,128)(2,1)}, u32[]{:S(2)}) copy-start(bf16[1,4096,128]{2,1,0:T(8,128)(2,1)} %k_hbm.1) | copy-start | bytes 3145732
  2.8 1.2 %copy-start.2 = (bf16[1,4096,128]{2,1,0:T(8,128)(2,1)S(1)}, bf16[1,4096,128]{2,1,0:T(8,128)(2,1)}, u32[]{:S(2)}) copy-start(bf16[1,4096,128]{2,1,0:T(8,128)(2,1)} %v_hbm.1) | copy-start | bytes 3145732

commit v2 on v1

--- a/solution.py
+++ b/solution.py
@@ -18,6 +18,10 @@
 REP = 8
 ROWS = 9
 FAR_FIRST = (8, 7, 9, 6, 10, 5, 11, 4, 12, 3, 13, 2, 14, 1, 15)
+PLANE = sorted(
+    ((dy, dx) for dy in range(4) for dx in range(4)),
+    key=lambda d: -(min(d[0], 4 - d[0]) + min(d[1], 4 - d[1])),
+)
 
 
 def split_two(value):
@@ -30,7 +34,7 @@
     query_count, key_count,
     q_hbm, k_hbm, v_hbm, out_ref,
     q_in, k_in, v_in, q_f32, packed, plane, line, part, full, weights, keys_t, scale,
-    expo, mass, in_sem, send_sem, recv_sem,
+    expo, mass, in_sem, send_sem, recv_sem, told,
 ):
     ctx = lax.axis_index("ctx")
     head = lax.axis_index("head")
@@ -41,24 +45,36 @@
     load_k = pltpu.make_async_copy(k_hbm, k_in, in_sem.at[1])
     load_v = pltpu.make_async_copy(v_hbm, v_in, in_sem.at[2])
     load_q.start()
+
+    plane_peers = [
+        (lax.rem(y + dy, NY), lax.rem(head + 2 * dx + dc, NH))
+        for dy, dx in PLANE
+        for dc in range(2)
+        if (dy, dx, dc) != (0, 0, 0)
+    ]
+    line_peers = [lax.rem(z + dz, NZ) for dz in FAR_FIRST]
+
+    barrier = pltpu.get_barrier_semaphore()
+    core = lax.rem(head, 2)
+    even = head - core
+    odd = even + 1
+
+    def greet(device):
+        pl.semaphore_signal(barrier, inc=1, device_id=device, device_id_type=MESH)
+
+    for dy, dx in PLANE:
+        if (dy, dx) != (0, 0):
+            greet((lax.rem(y + dy, NY) * NZ + z, lax.rem(odd + 2 * dx, NH)))
+    for zz in line_peers:
+        greet((y * NZ + zz, even))
+
+    @pl.when(core == 0)
+    def _():
+        greet((ctx, odd))
+
+    load_q.wait()
     load_k.start()
     load_v.start()
-
-    plane_peers = [
-        (lax.rem(y + dy, NY), lax.rem(head + dh, NH))
-        for dy in range(NY)
-        for dh in range(NH)
-        if (dy, dh) != (0, 0)
-    ]
-    line_peers = [lax.rem(z + dz, NZ) for dz in FAR_FIRST]
-
-    barrier = pltpu.get_barrier_semaphore()
-    for zz in line_peers:
-        pl.semaphore_signal(barrier, inc=1, device_id=(y * NZ + zz, head), device_id_type=MESH)
-    for yy, hh in plane_peers:
-        pl.semaphore_signal(barrier, inc=1, device_id=(yy * NZ + z, hh), device_id_type=MESH)
-
-    load_q.wait()
     step = 64
 
     def widen(t, _):
@@ -87,7 +103,14 @@
             packed[g, q, 0, 8:9, :] = first
             packed[g, q, 1, 8:9, :] = diagonal
 
-    pl.semaphore_wait(barrier, len(plane_peers) + len(line_peers))
+    @pl.when(core == 1)
+    def _():
+        pl.semaphore_wait(barrier, 31)
+        pl.semaphore_signal(told, inc=1, device_id=(ctx, even), device_id_type=MESH)
+
+    @pl.when(core == 0)
+    def _():
+        pl.semaphore_wait(told, 1)
 
     def copy(src, dst, phase, device):
         return pltpu.make_async_remote_copy(
@@ -117,11 +140,20 @@
 
     lax.fori_loop(0, key_count // wide, turn_keys, 0)
 
+    @pl.when(core == 0)
+    def _():
+        pl.semaphore_wait(barrier, 30)
+        pl.semaphore_signal(told, inc=1, device_id=(ctx, odd), device_id_type=MESH)
+
     wait(plane.at[pl.ds(0, 62), pl.ds(0, ROWS)], recv_sem.at[0])
     total = plane[0:16, 0:ROWS, :]
     for yy in range(1, NY):
         total = total + plane[yy * 16 : yy * 16 + 16, 0:ROWS, :]
     line[:, 0:ROWS, :] = total
+
+    @pl.when(core == 1)
+    def _():
+        pl.semaphore_wait(told, 1)
 
     for zz in line_peers:
         copy(line.at[zz, pl.ds(0, ROWS)], part.at[z, pl.ds(0, ROWS)], 1, (y * NZ + zz, head)).start()
@@ -178,19 +210,15 @@
     weights[REP * DH : REP * DH + 16, 0:DH] = high
     weights[REP * DH : REP * DH + 16, DH : 2 * DH] = low
 
-    tile = 256
-
-    def score(t, _):
-        keys = keys_t[:, pl.ds(t * tile, tile)]
+    tile = 512
+    for t in range(key_count // tile):
+        keys = keys_t[:, t * tile : (t + 1) * tile]
         keys_f32 = keys[0:DH].astype(F32)
         projected = jnp.dot(weights[...], keys, preferred_element_type=F32)
         for r in range(REP):
             quadratic = jnp.sum(projected[r * DH : (r + 1) * DH] * keys_f32, axis=0, keepdims=True)
             linear = projected[REP * DH + 2 * r : REP * DH + 2 * r + 1]
-            expo[r : r + 1, pl.ds(t * tile, tile)] = quadratic + linear
-        return 0
-
-    lax.fori_loop(0, key_count // tile, score, 0)
+            expo[r : r + 1, t * tile : (t + 1) * tile] = quadratic + linear
 
     exponent = expo[...]
     peak = jnp.max(exponent, axis=1, keepdims=True)
@@ -230,7 +258,7 @@
 def local(query_rows, key_rows, value_rows):
     query_count = query_rows.shape[1]
     key_count = key_rows.shape[1]
-    any_space = pl.BlockSpec(memory_space=pl.ANY)
+    any_space = pl.BlockSpec(memory_space=pltpu.HBM)
     return pl.pallas_call(
         functools.partial(kernel, query_count, key_count),
         out_shape=jax.ShapeDtypeStruct((1, key_count), F32),
@@ -254,9 +282,10 @@
             pltpu.SemaphoreType.DMA((3,)),
             pltpu.SemaphoreType.DMA((5,)),
             pltpu.SemaphoreType.DMA((5,)),
+            pltpu.SemaphoreType.REGULAR,
         ],
         compiler_params=pltpu.CompilerParams(
-            collective_id=0, has_side_effects=True, vmem_limit_bytes=48 << 20
+            collective_id=0, has_side_effects=True, vmem_limit_bytes=62 << 20
         ),
     )(query_rows, key_rows, value_rows)
 

time: 60.6 us -> 52.8 us (0.87)
  Pallas kernels: 55.6 us -> 51.3 us
  local copies, waits for them, and re-layouts: 4.65 us -> 1.32 us
    pallas_call x1, Pallas kernels: 55.6 us -> 51.3 us  [local(): pl.pallas_call(functools.partial(kernel, query_count, key_count), out_sha...]
    unnamed x7 -> x1, local copies, waits for them, and re-layouts: 4.65 us -> 1.32 us
where the time goes in v2:
time: 52.8 us; the launch traced here: 52.6 us
  Pallas kernels  51.3 us (97%)
  local copies, waits for them, and re-layouts  1.32 us (2%)
    pallas_call x1, Pallas kernels, local(): pl.pallas_call(functools.partial(kernel, query_count, key_count), out_sha...  51.3 us
    unnamed x1, local copies, waits for them, and re-layouts  1.32 us

profile of v2, /device:TPU:2, one launch (start us, length us, event | category | flops | bytes accessed | tf_op | source)
XLA Modules:
  0.0 52.6 jit_solution(11631122011675120487)
XLA Ops:
  0.0 51.3 %shard_map.37 = f32[1,4096]{1,0:T(1,128)} custom-call(bf16[1,1024,8,128]{3,2,1,0:T(8,128)(2,1)} %q_hbm.1, bf16[1,4096,128]{2,1,0:T(8,128)(2,1)} %k_hbm.1, bf16[1,4096,128]{2,1,0:T(8,128)(2,1)} %v_hbm.1), custom_call_target="tpu_custom_call" | custom-call | tf_op jit(solution)/shard_map/pallas_call | solution.py:262
  51.3 1.3 %copy.5 = f32[1,4096]{1,0:T(1,128)} copy(f32[1,4096]{1,0:T(1,128)} %shard_map.37) | data formatting | bytes 32768

commit v3 on v2

--- a/solution.py
+++ b/solution.py
@@ -18,6 +18,9 @@
 REP = 8
 ROWS = 9
 FAR_FIRST = (8, 7, 9, 6, 10, 5, 11, 4, 12, 3, 13, 2, 14, 1, 15)
+FAR = (8, 7, 9, 6, 10)
+NEAR = (5, 11, 4, 12, 3, 13, 2, 14, 1, 15)
+ORDER = (0, 1, 2, 6, 7, 3, 4, 5)
 PLANE = sorted(
     ((dy, dx) for dy in range(4) for dx in range(4)),
     key=lambda d: -(min(d[0], 4 - d[0]) + min(d[1], 4 - d[1])),
@@ -176,25 +179,44 @@
     mine = y * 16 + z
     full[mine, 0:ROWS, :] = total
 
-    for zz in line_peers:
-        here = full.at[mine, pl.ds(0, ROWS)]
-        copy(here, here, 2, (y * NZ + zz, head)).start()
-    wait(full.at[pl.ds(0, 15), pl.ds(0, ROWS)], recv_sem.at[2])
-
-    for dy in range(1, NY):
-        here = full.at[pl.ds(y * 16, 16), pl.ds(0, 8)]
-        copy(here, here, 3, (lax.rem(y + dy, NY) * NZ + z, head)).start()
-    extra = full[pl.ds(y * 16, 16), 8, :] * (1.0 / (query_count * NY * NZ))
+    def along_z(dz):
+        return y * NZ + lax.rem(z + dz, NZ)
+
+    here = full.at[mine, pl.ds(0, ROWS)]
+    for dz in FAR:
+        copy(here, here, 2, (along_z(dz), head)).start()
+    for dz in NEAR:
+        copy(here, here, 3, (along_z(dz), head)).start()
+
+    def pass_on(dz, phase):
+        there = full.at[along_z(dz), pl.ds(0, 8)]
+        for dy in (2, 1, 3):
+            copy(there, there, phase, (lax.rem(y + dy, NY) * NZ + z, head)).start()
+
+    pass_on(0, 4)
+    wait(full.at[pl.ds(0, len(NEAR)), pl.ds(0, ROWS)], recv_sem.at[3])
+    for dz in NEAR:
+        pass_on(dz, 4)
+    wait(full.at[pl.ds(0, len(FAR)), pl.ds(0, ROWS)], recv_sem.at[2])
+    for dz in FAR:
+        pass_on(dz, 5)
+
+    base = lax.div(z, 2)
+    order = [lax.rem(base + k, REP) for k in ORDER]
+    extra = jnp.concatenate(
+        [full[y * 16 + 2 * r + h, 8:9, :] for r in order for h in range(2)], axis=0
+    ) * (1.0 / (query_count * NY * NZ))
     columns = extra.T
-    wait(full.at[pl.ds(0, 48), pl.ds(0, 8)], recv_sem.at[3])
-
-    for r in range(REP):
+    linear_rows = split_two(extra * (1.0 / math.sqrt(DH)))
+
+    def weigh(p, at):
+        r = order[p]
         quarters = [full[q * 16 + 2 * r + h, 0:8, :] for q in range(NY) for h in range(2)]
         moments = jnp.concatenate(quarters, axis=0) * (1.0 / (query_count * NY * NZ))
-        center = extra[2 * r : 2 * r + 1, :]
-        up = columns[0:HALF, 2 * r : 2 * r + 1]
-        down = columns[HALF:DH, 2 * r : 2 * r + 1]
-        diagonal = columns[0:HALF, 2 * r + 1 : 2 * r + 2]
+        center = extra[2 * p : 2 * p + 1, :]
+        up = columns[0:HALF, 2 * p : 2 * p + 1]
+        down = columns[HALF:DH, 2 * p : 2 * p + 1]
+        diagonal = columns[0:HALF, 2 * p + 1 : 2 * p + 2]
         below = lane < row
         value = moments - jnp.where(below, down * pltpu.roll(center, HALF, 1), up * center)
         value = value * (1.0 / (2.0 * DH))
@@ -202,23 +224,36 @@
         on = lane == row
         upper = jnp.where(below, 0.0, jnp.where(on, value, 2.0 * value))
         lower = jnp.where(below, 2.0 * value, jnp.where(on, corner, 0.0))
-        for at, block in ((0, upper), (HALF, pltpu.roll(lower, HALF, 1))):
+        for block in (upper, pltpu.roll(lower, HALF, 1)):
             high, low = split_two(block)
-            weights[r * DH + at : r * DH + at + HALF, 0:DH] = high
-            weights[r * DH + at : r * DH + at + HALF, DH : 2 * DH] = low
-    high, low = split_two(extra * (1.0 / math.sqrt(DH)))
-    weights[REP * DH : REP * DH + 16, 0:DH] = high
-    weights[REP * DH : REP * DH + 16, DH : 2 * DH] = low
+            weights[at : at + HALF, 0:DH] = high
+            weights[at : at + HALF, DH : 2 * DH] = low
+            at += HALF
 
     tile = 512
-    for t in range(key_count // tile):
-        keys = keys_t[:, t * tile : (t + 1) * tile]
-        keys_f32 = keys[0:DH].astype(F32)
-        projected = jnp.dot(weights[...], keys, preferred_element_type=F32)
-        for r in range(REP):
-            quadratic = jnp.sum(projected[r * DH : (r + 1) * DH] * keys_f32, axis=0, keepdims=True)
-            linear = projected[REP * DH + 2 * r : REP * DH + 2 * r + 1]
-            expo[r : r + 1, t * tile : (t + 1) * tile] = quadratic + linear
+
+    def score(members, at):
+        end = at + len(members) * DH
+        for i, p in enumerate(members):
+            weigh(p, at + i * DH)
+        weights[end : end + 16, 0:DH] = linear_rows[0]
+        weights[end : end + 16, DH : 2 * DH] = linear_rows[1]
+        for t in range(key_count // tile):
+            keys = keys_t[:, t * tile : (t + 1) * tile]
+            keys_f32 = keys[0:DH].astype(F32)
+            projected = jnp.dot(weights[at : end + 16, :], keys, preferred_element_type=F32)
+            for i, p in enumerate(members):
+                quadratic = jnp.sum(
+                    projected[i * DH : (i + 1) * DH] * keys_f32, axis=0, keepdims=True
+                )
+                linear = projected[end - at + 2 * p : end - at + 2 * p + 1]
+                expo[p : p + 1, t * tile : (t + 1) * tile] = quadratic + linear
+
+    near_heads, far_heads = range(0, 5), range(5, REP)
+    wait(full.at[pl.ds(0, 3 * (1 + len(NEAR))), pl.ds(0, 8)], recv_sem.at[4])
+    score(near_heads, 0)
+    wait(full.at[pl.ds(0, 3 * len(FAR)), pl.ds(0, 8)], recv_sem.at[5])
+    score(far_heads, 5 * DH + 16)
 
     exponent = expo[...]
     peak = jnp.max(exponent, axis=1, keepdims=True)
@@ -227,21 +262,23 @@
     local = jnp.sum(grown, axis=1, keepdims=True)
     row8 = lax.broadcasted_iota(jnp.int32, (REP, DH), 0)
     lane8 = lax.broadcasted_iota(jnp.int32, (REP, DH), 1)
-    note = jnp.where(lane8 == row8, peak, jnp.where(lane8 == row8 + REP, local, 0.0))
+    place = jnp.where(row8 < 3, row8, jnp.where(row8 < 5, row8 + 3, row8 - 2))
+    place = lax.rem(place + base, REP)
+    note = jnp.where(lane8 == place, peak, jnp.where(lane8 == place + REP, local, 0.0))
     mass[pl.ds(ctx, 1), :] = jnp.sum(note, axis=0, keepdims=True)
     for dz in FAR_FIRST + (0,):
         for dy in (2, 1, 3, 0):
             if (dy, dz) != (0, 0):
                 here = mass.at[pl.ds(ctx, 1)]
-                copy(here, here, 4, (lax.rem(y + dy, NY) * NZ + lax.rem(z + dz, NZ), head)).start()
-    wait(mass.at[pl.ds(0, 63)], recv_sem.at[4])
+                copy(here, here, 6, (lax.rem(y + dy, NY) * NZ + lax.rem(z + dz, NZ), head)).start()
+    wait(mass.at[pl.ds(0, 63)], recv_sem.at[6])
     notes = mass[...]
     highest = jnp.max(notes, axis=0, keepdims=True)
     sums = pltpu.roll(notes, DH - REP, 1)
     inside = lax.broadcasted_iota(jnp.int32, notes.shape, 1) < REP
     terms = jnp.where(inside, sums * jnp.exp(jnp.where(inside, notes - highest, 0.0)), 0.0)
     denominator = jnp.sum(terms, axis=0, keepdims=True)
-    pick = lane8 == row8
+    pick = lane8 == place
     highest_col = jnp.sum(jnp.where(pick, highest, 0.0), axis=1, keepdims=True)
     denominator_col = jnp.sum(jnp.where(pick, denominator, 0.0), axis=1, keepdims=True)
     factor = jnp.exp(peak - highest_col) / denominator_col
@@ -250,9 +287,11 @@
 
     wait(plane.at[pl.ds(0, 62), pl.ds(0, ROWS)], send_sem.at[0])
     wait(part.at[pl.ds(0, 15), pl.ds(0, ROWS)], send_sem.at[1])
-    wait(full.at[pl.ds(0, 15), pl.ds(0, ROWS)], send_sem.at[2])
-    wait(full.at[pl.ds(0, 48), pl.ds(0, 8)], send_sem.at[3])
-    wait(mass.at[pl.ds(0, 63)], send_sem.at[4])
+    wait(full.at[pl.ds(0, len(FAR)), pl.ds(0, ROWS)], send_sem.at[2])
+    wait(full.at[pl.ds(0, len(NEAR)), pl.ds(0, ROWS)], send_sem.at[3])
+    wait(full.at[pl.ds(0, 3 * (1 + len(NEAR))), pl.ds(0, 8)], send_sem.at[4])
+    wait(full.at[pl.ds(0, 3 * len(FAR)), pl.ds(0, 8)], send_sem.at[5])
+    wait(mass.at[pl.ds(0, 63)], send_sem.at[6])
 
 
 def local(query_rows, key_rows, value_rows):
@@ -274,14 +313,14 @@
             pltpu.VMEM((NZ, 16, DH), F32),
             pltpu.VMEM((NZ, 16, DH), F32),
             pltpu.VMEM((NY * 16, 16, DH), F32),
-            pltpu.VMEM((REP * DH + 16, 2 * DH), BF16),
+            pltpu.VMEM((REP * DH + 32, 2 * DH), BF16),
             pltpu.VMEM((2 * DH, key_count), BF16),
             pltpu.VMEM((1, key_count), F32),
             pltpu.VMEM((REP, key_count), F32),
             pltpu.VMEM((NY * NZ, DH), F32),
             pltpu.SemaphoreType.DMA((3,)),
-            pltpu.SemaphoreType.DMA((5,)),
-            pltpu.SemaphoreType.DMA((5,)),
+            pltpu.SemaphoreType.DMA((7,)),
+            pltpu.SemaphoreType.DMA((7,)),
             pltpu.SemaphoreType.REGULAR,
         ],
         compiler_params=pltpu.CompilerParams(

time: 52.8 us -> 51.3 us (0.972)
  the two profiles are of different devices: /device:TPU:2 before, /device:TPU:8 now
where the time goes in v3:
time: 51.3 us; the launch traced here: 51.1 us
  Pallas kernels  49.8 us (97%)
  local copies, waits for them, and re-layouts  1.32 us (3%)
    pallas_call x1, Pallas kernels, local(): pl.pallas_call(functools.partial(kernel, query_count, key_count), out_sha...  49.8 us
    unnamed x1, local copies, waits for them, and re-layouts  1.32 us

profile of v3, /device:TPU:8, one launch (start us, length us, event | category | flops | bytes accessed | tf_op | source)
XLA Modules:
  0.0 51.1 jit_solution(2226550594993543222)
XLA Ops:
  0.0 49.8 %shard_map.37 = f32[1,4096]{1,0:T(1,128)} custom-call(bf16[1,1024,8,128]{3,2,1,0:T(8,128)(2,1)} %q_hbm.1, bf16[1,4096,128]{2,1,0:T(8,128)(2,1)} %k_hbm.1, bf16[1,4096,128]{2,1,0:T(8,128)(2,1)} %v_hbm.1), custom_call_target="tpu_custom_call" | custom-call | tf_op jit(solution)/shard_map/pallas_call | solution.py:301
  49.8 1.3 %copy.5 = f32[1,4096]{1,0:T(1,128)} copy(f32[1,4096]{1,0:T(1,128)} %shard_map.37) | data formatting | bytes 32768

commit v4 on v3

--- a/solution.py
+++ b/solution.py
@@ -20,7 +20,6 @@
 FAR_FIRST = (8, 7, 9, 6, 10, 5, 11, 4, 12, 3, 13, 2, 14, 1, 15)
 FAR = (8, 7, 9, 6, 10)
 NEAR = (5, 11, 4, 12, 3, 13, 2, 14, 1, 15)
-ORDER = (0, 1, 2, 6, 7, 3, 4, 5)
 PLANE = sorted(
     ((dy, dx) for dy in range(4) for dx in range(4)),
     key=lambda d: -(min(d[0], 4 - d[0]) + min(d[1], 4 - d[1])),
@@ -36,7 +35,7 @@
 def kernel(
     query_count, key_count,
     q_hbm, k_hbm, v_hbm, out_ref,
-    q_in, k_in, v_in, q_f32, packed, plane, line, part, full, weights, keys_t, scale,
+    q_in, k_in, v_in, q_f32, packed, plane, line, part, full, columns, weights, keys_t, scale,
     expo, mass, in_sem, send_sem, recv_sem, told,
 ):
     ctx = lax.axis_index("ctx")
@@ -167,7 +166,8 @@
     def scale_values(t, _):
         turned = v_in[0, pl.ds(t * wide, wide), :].astype(F32).T
         squares = jnp.sum(turned * turned, axis=0, keepdims=True)
-        scale[:, pl.ds(t * wide, wide)] = jnp.sqrt(squares / DH + 1e-06)
+        values = jnp.sqrt(squares / DH + 1e-06) * (key_count * NY * NZ / REP)
+        scale[:, pl.ds(t * wide, wide)] = values
         return 0
 
     lax.fori_loop(0, key_count // wide, scale_values, 0)
@@ -201,70 +201,90 @@
     for dz in FAR:
         pass_on(dz, 5)
 
-    base = lax.div(z, 2)
-    order = [lax.rem(base + k, REP) for k in ORDER]
-    extra = jnp.concatenate(
-        [full[y * 16 + 2 * r + h, 8:9, :] for r in order for h in range(2)], axis=0
-    ) * (1.0 / (query_count * NY * NZ))
-    columns = extra.T
-    linear_rows = split_two(extra * (1.0 / math.sqrt(DH)))
-
-    def weigh(p, at):
-        r = order[p]
-        quarters = [full[q * 16 + 2 * r + h, 0:8, :] for q in range(NY) for h in range(2)]
-        moments = jnp.concatenate(quarters, axis=0) * (1.0 / (query_count * NY * NZ))
-        center = extra[2 * p : 2 * p + 1, :]
-        up = columns[0:HALF, 2 * p : 2 * p + 1]
-        down = columns[HALF:DH, 2 * p : 2 * p + 1]
-        diagonal = columns[0:HALF, 2 * p + 1 : 2 * p + 2]
-        below = lane < row
-        value = moments - jnp.where(below, down * pltpu.roll(center, HALF, 1), up * center)
-        value = value * (1.0 / (2.0 * DH))
-        corner = (diagonal - down * down) * (1.0 / (2.0 * DH))
-        on = lane == row
-        upper = jnp.where(below, 0.0, jnp.where(on, value, 2.0 * value))
-        lower = jnp.where(below, 2.0 * value, jnp.where(on, corner, 0.0))
-        for block in (upper, pltpu.roll(lower, HALF, 1)):
-            high, low = split_two(block)
-            weights[at : at + HALF, 0:DH] = high
-            weights[at : at + HALF, DH : 2 * DH] = low
-            at += HALF
+    extra = full[pl.ds(y * 16, 16), 8, :] * (1.0 / (query_count * NY * NZ))
+    columns[:, 0:16] = extra.T
+    row16 = lax.broadcasted_iota(jnp.int32, (16, DH), 0)
+    lane16 = lax.broadcasted_iota(jnp.int32, (16, DH), 1)
+
+    def quarter(dq):
+        return lax.rem(y + dq, NY)
+
+    def sixteen(start):
+        return pl.ds(pl.multiple_of(start, 16), 16)
+
+    def weigh(dq, at):
+        q = quarter(dq)
+        ups = columns[sixteen(q * 16), 0:16]
+        downs = columns[sixteen(HALF + q * 16), 0:16]
+        below = lane16 < row16 + q * 16
+        on = lane16 == row16 + q * 16
+        for r in range(REP):
+            moments = jnp.concatenate(
+                [full[q * 16 + 2 * r + h, 0:8, :] for h in range(2)], axis=0
+            ) * (1.0 / (query_count * NY * NZ))
+            center = extra[2 * r : 2 * r + 1, :]
+            up = ups[:, 2 * r : 2 * r + 1]
+            down = downs[:, 2 * r : 2 * r + 1]
+            diagonal = ups[:, 2 * r + 1 : 2 * r + 2]
+            value = moments - jnp.where(below, down * pltpu.roll(center, HALF, 1), up * center)
+            value = value * (1.0 / (2.0 * DH))
+            corner = (diagonal - down * down) * (1.0 / (2.0 * DH))
+            upper = jnp.where(below, 0.0, jnp.where(on, value, 2.0 * value))
+            lower = jnp.where(below, 2.0 * value, jnp.where(on, corner, 0.0))
+            for start, block in ((at, upper), (at + REP * 16, pltpu.roll(lower, HALF, 1))):
+                high, low = split_two(block)
+                start += r * 16
+                weights[start : start + 16, 0:DH] = high
+                weights[start : start + 16, DH : 2 * DH] = low
 
     tile = 512
-
-    def score(members, at):
-        end = at + len(members) * DH
-        for i, p in enumerate(members):
-            weigh(p, at + i * DH)
-        weights[end : end + 16, 0:DH] = linear_rows[0]
-        weights[end : end + 16, DH : 2 * DH] = linear_rows[1]
-        for t in range(key_count // tile):
-            keys = keys_t[:, t * tile : (t + 1) * tile]
-            keys_f32 = keys[0:DH].astype(F32)
-            projected = jnp.dot(weights[at : end + 16, :], keys, preferred_element_type=F32)
-            for i, p in enumerate(members):
-                quadratic = jnp.sum(
-                    projected[i * DH : (i + 1) * DH] * keys_f32, axis=0, keepdims=True
-                )
-                linear = projected[end - at + 2 * p : end - at + 2 * p + 1]
-                expo[p : p + 1, t * tile : (t + 1) * tile] = quadratic + linear
-
-    near_heads, far_heads = range(0, 5), range(5, REP)
+    tiles = [pl.ds(t * tile, tile) for t in range(key_count // tile)]
+    rows_of = 2 * REP * 16
+
+    def score(quarters, at, end, span):
+        keys = keys_t[:, span]
+        projected = jnp.dot(weights[at:end, :], keys, preferred_element_type=F32)
+        totals = [0.0] * REP
+        for i, dq in enumerate(quarters):
+            for half in range(2):
+                some = keys_t[sixteen(half * HALF + quarter(dq) * 16), span].astype(F32)
+                for r in range(REP):
+                    start = i * rows_of + (half * REP + r) * 16
+                    totals[r] = totals[r] + projected[start : start + 16] * some
+        return [jnp.sum(v, axis=0, keepdims=True) for v in totals], projected
+
+    weigh(0, 0)
+    high, low = split_two(extra * (1.0 / math.sqrt(DH)))
+    weights[rows_of : rows_of + 16, 0:DH] = high
+    weights[rows_of : rows_of + 16, DH : 2 * DH] = low
+    for span in tiles:
+        totals, projected = score((0,), 0, rows_of + 16, span)
+        for r in range(REP):
+            linear = projected[rows_of + 2 * r : rows_of + 2 * r + 1]
+            expo[r : r + 1, span] = totals[r] + linear
+
     wait(full.at[pl.ds(0, 3 * (1 + len(NEAR))), pl.ds(0, 8)], recv_sem.at[4])
-    score(near_heads, 0)
     wait(full.at[pl.ds(0, 3 * len(FAR)), pl.ds(0, 8)], recv_sem.at[5])
-    score(far_heads, 5 * DH + 16)
-
-    exponent = expo[...]
-    peak = jnp.max(exponent, axis=1, keepdims=True)
-    grown = jnp.exp(exponent - peak)
-    expo[...] = grown
-    local = jnp.sum(grown, axis=1, keepdims=True)
+    for dq in range(1, NY):
+        weigh(dq, rows_of * dq + 16)
+    tops, sums = [], []
+    for span in tiles:
+        totals, _ = score((1, 2, 3), rows_of + 16, NY * rows_of + 16, span)
+        for r in range(REP):
+            expo[r : r + 1, span] = expo[r : r + 1, span] + totals[r]
+        pieces = jnp.split(expo[:, span], tile // DH, axis=1)
+        top = functools.reduce(jnp.maximum, pieces)
+        pieces = [jnp.exp(piece - top) for piece in pieces]
+        expo[:, span] = jnp.concatenate(pieces, axis=1)
+        tops.append(top)
+        sums.append(functools.reduce(jnp.add, pieces))
+
+    peak = jnp.max(functools.reduce(jnp.maximum, tops), axis=1, keepdims=True)
+    lifts = [jnp.exp(top - peak) for top in tops]
+    local = jnp.sum(sum(v * f for v, f in zip(sums, lifts)), axis=1, keepdims=True)
     row8 = lax.broadcasted_iota(jnp.int32, (REP, DH), 0)
     lane8 = lax.broadcasted_iota(jnp.int32, (REP, DH), 1)
-    place = jnp.where(row8 < 3, row8, jnp.where(row8 < 5, row8 + 3, row8 - 2))
-    place = lax.rem(place + base, REP)
-    note = jnp.where(lane8 == place, peak, jnp.where(lane8 == place + REP, local, 0.0))
+    note = jnp.where(lane8 == row8, peak, jnp.where(lane8 == row8 + REP, local, 0.0))
     mass[pl.ds(ctx, 1), :] = jnp.sum(note, axis=0, keepdims=True)
     for dz in FAR_FIRST + (0,):
         for dy in (2, 1, 3, 0):
@@ -278,12 +298,14 @@
     inside = lax.broadcasted_iota(jnp.int32, notes.shape, 1) < REP
     terms = jnp.where(inside, sums * jnp.exp(jnp.where(inside, notes - highest, 0.0)), 0.0)
     denominator = jnp.sum(terms, axis=0, keepdims=True)
-    pick = lane8 == place
+    pick = lane8 == row8
     highest_col = jnp.sum(jnp.where(pick, highest, 0.0), axis=1, keepdims=True)
     denominator_col = jnp.sum(jnp.where(pick, denominator, 0.0), axis=1, keepdims=True)
     factor = jnp.exp(peak - highest_col) / denominator_col
-    share = jnp.sum(expo[...] * factor, axis=0, keepdims=True)
-    out_ref[...] = share * scale[...] * (key_count * NY * NZ / REP)
+    for span, lift in zip(tiles, lifts):
+        weight = jnp.concatenate([lift * factor] * (tile // DH), axis=1)
+        share = jnp.sum(expo[:, span] * weight, axis=0, keepdims=True)
+        out_ref[:, span] = share * scale[:, span]
 
     wait(plane.at[pl.ds(0, 62), pl.ds(0, ROWS)], send_sem.at[0])
     wait(part.at[pl.ds(0, 15), pl.ds(0, ROWS)], send_sem.at[1])
@@ -313,7 +335,8 @@
             pltpu.VMEM((NZ, 16, DH), F32),
             pltpu.VMEM((NZ, 16, DH), F32),
             pltpu.VMEM((NY * 16, 16, DH), F32),
-            pltpu.VMEM((REP * DH + 32, 2 * DH), BF16),
+            pltpu.VMEM((DH, DH), F32),
+            pltpu.VMEM((REP * DH + 16, 2 * DH), BF16),
             pltpu.VMEM((2 * DH, key_count), BF16),
             pltpu.VMEM((1, key_count), F32),
             pltpu.VMEM((REP, key_count), F32),
@@ -324,7 +347,7 @@
             pltpu.SemaphoreType.REGULAR,
         ],
         compiler_params=pltpu.CompilerParams(
-            collective_id=0, has_side_effects=True, vmem_limit_bytes=62 << 20
+            collective_id=0, has_side_effects=True, vmem_limit_bytes=53 << 20
         ),
     )(query_rows, key_rows, value_rows)
 

time: 51.3 us -> 49.7 us (0.969)
  the two profiles are of different devices: /device:TPU:8 before, /device:TPU:2 now
where the time goes in v4:
time: 49.7 us; the launch traced here: 49.6 us
  Pallas kernels  48.9 us (98%)
  local copies, waits for them, and re-layouts  0.61 us (1%)
    pallas_call x1, Pallas kernels, local(): pl.pallas_call(functools.partial(kernel, query_count, key_count), out_sha...  48.9 us

profile of v4, /device:TPU:2, one launch (start us, length us, event | category | flops | bytes accessed | tf_op | source)
XLA Modules:
  0.0 49.6 jit_solution(6526987817142870941)
XLA Ops:
  0.0 48.9 %shard_map.37 = f32[1,4096]{1,0:T(1,128)S(1)} custom-call(bf16[1,1024,8,128]{3,2,1,0:T(8,128)(2,1)} %q_hbm.1, bf16[1,4096,128]{2,1,0:T(8,128)(2,1)} %k_hbm.1, bf16[1,4096,128]{2,1,0:T(8,128)(2,1)} %v_hbm.1), custom_call_target="tpu_custom_call" | custom-call | tf_op jit(solution)/shard_map/pallas_call | solution.py:323
  49.0 0.6 %copy.5 = f32[1,4096]{1,0:T(1,128)} copy(f32[1,4096]{1,0:T(1,128)S(1)} %shard_map.37) | data formatting | bytes 32768
